TPU v7x, 1024 devices: a whole 4x4x32 slice. The times are simulated.
1024 devices in a mesh: replica: 64 (over x, z_lo), fsdp: 16 (over y, z_hi, core).
Axes of the slice: x: 4, y: 4, z: 32 (z_hi: 2, z_lo: 16; z = z_hi * 16 + z_lo), core: 2. Of those that a mesh axis runs over, the one named last changes fastest.
Arguments:
- local_weights: bfloat16 [64, 256, 8192], P('replica', 'fsdp'), may hold values from -16 to 16
- base_weights: float32 [256, 8192], P('fsdp'), may hold values from -6 to 6
- momentum: float32 [256, 8192], P('fsdp', 'replica'), may hold values from -6 to 6
Outputs:
- merged_fragment: bfloat16 [64, 256, 8192], P('replica')
- new_base: float32 [256, 8192], P('fsdp', 'replica')
- new_momentum: float32 [256, 8192], P('fsdp', 'replica')
All inputs are finite; a program needn't handle non-finite values.
Results may differ from a plain program's by a relative error of at most 0.0055.
Values may be sent and summed in bfloat16 or wider, within the bound.
A program may use at most 32 MiB of HBM per device.

v0:
```python
import jax
import jax.numpy as jnp
from jax import lax
from jax.sharding import PartitionSpec as P

D = 8192
BLOCK = 32


def encode(delta):
    rows = delta.shape[0]
    blocks = delta.reshape(rows, D // BLOCK, BLOCK)
    largest = jnp.max(jnp.abs(blocks), axis=2)
    scale = (jnp.maximum(largest, 1.0) / 6.0).astype(jnp.bfloat16)
    ratio = blocks / scale.astype(jnp.float32)[:, :, None]
    codes = jnp.clip(ratio, -4.0, 4.0).astype(jnp.bfloat16)
    return (codes, scale)


def per_device(local_weights, base_weights, momentum):
    replicas = lax.axis_size("replica")
    owned = D // replicas
    rows_here = base_weights.shape[0]
    local_rows = local_weights[0]
    delta = base_weights - local_rows.astype(jnp.float32)
    codes, scale = encode(delta)
    decoded = (codes.astype(jnp.float32) * scale.astype(jnp.float32)[:, :, None]).reshape(
        rows_here, D
    )
    total = lax.psum_scatter(decoded, "replica", scatter_dimension=1, tiled=True)
    grad = total / replicas
    start = lax.axis_index("replica") * owned
    base_owned = lax.dynamic_slice_in_dim(base_weights, start, owned, 1)
    new_momentum = 0.9 * momentum + grad
    new_base = base_owned - 0.7 * (grad + 0.9 * new_momentum)
    full_base = lax.all_gather(new_base, "replica", axis=1, tiled=True)
    blended = (0.5 * full_base + 0.5 * local_rows.astype(jnp.float32)).astype(jnp.bfloat16)
    merged_fragment = lax.all_gather(blended, "fsdp", axis=0, tiled=True)
    return (merged_fragment[None], new_base, new_momentum)


def solution(mesh):
    in_specs = (P("replica", "fsdp", None), P("fsdp", None), P("fsdp", "replica"))
    out_specs = (P("replica", None, None), P("fsdp", "replica"), P("fsdp", "replica"))
    return jax.shard_map(
        per_device, mesh=mesh, in_specs=in_specs, out_specs=out_specs, check_vma=False
    )
```

profile of v0, /device:TPU:1, one launch (start us, length us, event | category | flops | bytes accessed | tf_op | source)
XLA Modules:
  0.0 1402.1 jit_solution(6455264212881279912)
XLA Ops:
  7.2 0.0 reduce-scatter.2.cloned.1.call-start
  7.2 1.2 fusion.2
  8.4 0.0 copy-start
  8.4 0.0 copy-start.1
  8.4 0.7 abs.7
  9.1 0.0 copy-start.3
  9.1 0.6 reduce_max.9
  9.7 0.6 div.25
  10.3 1.0 div.26
  11.3 0.0 copy-done
  11.3 0.0 copy-done.1
  11.3 0.9 convert_multiply_fusion
  12.2 0.0 reduce-scatter.2.cloned.1.call-update
  12.3 0.0 all-gather.2.cloned.1.call-start
  12.3 738.0 %reduce-scatter.2.cloned.1.call-done = f32[16,128]{1,0:T(8,128)} async-done(((f32[16,8192]{1,0:T(8,128)}), f32[16,128]{1,0:T(8,128)}) %reduce-scatter.2.cloned.1.call-update) | async-done | bytes 8208 | tf_op jit(solution)/shard_map/reduce_scatter | solution.py:30
  750.3 0.0 copy-done.3
  750.3 1.3 multiply_subtract_fusion
  751.6 0.0 copy-start.2
  751.6 353.0 %all_gather.6 = f32[16,8192]{1,0:T(8,128)S(1)} all-gather(f32[16,128]{1,0:T(8,128)S(1)} %get-tuple-element.9), channel_id=1, replica_groups=mesh['replica'=64,'fsdp'=16] {'replica'}, dimensions={1}, use_global_device_ids=true | all-gather | bytes 532480 | tf_op jit(solution)/shard_map/all_gather | solution.py:36
  1104.6 0.8 fusion.1
  1105.4 0.0 all-gather.2.cloned.1.call-update
  1105.4 285.2 %all-gather.2.cloned.1.call-done = bf16[256,8192]{1,0:T(8,128)(2,1)} async-done(((bf16[16,8192]{1,0:T(8,128)(2,1)}), bf16[256,8192]{1,0:T(8,128)(2,1)}) %all-gather.2.cloned.1.call-update) | async-done | bytes 4194320 | tf_op jit(solution)/shard_map/all_gather | solution.py:38
  1390.6 4.6 copy.7
  1395.3 0.0 copy-done.2
  (1 shorter events, 0.0 us)
Async XLA Ops:
  7.2 743.2 %reduce-scatter.2.cloned.1.call-start = ((), (), s32[]{:S(2)}) async-start(), calls=%async_computation.1 | async-start | bytes 532480 | tf_op jit(solution)/shard_map/reduce_scatter | solution.py:30
  8.4 2.9 copy-start
  8.4 2.9 copy-start.1
  9.1 741.2 %copy-start.3 = (f32[16,128]{1,0:T(8,128)S(1)}, f32[16,128]{1,0:T(8,128)}, u32[]{:S(2)}) copy-start(f32[16,128]{1,0:T(8,128)} %param.5) | copy-start | bytes 24580
  12.3 1378.4 %all-gather.2.cloned.1.call-start = ((), (), s32[]{:S(2)}) async-start(), calls=%async_computation.2 | async-start | bytes 4456448 | tf_op jit(solution)/shard_map/all_gather | solution.py:38
  751.6 643.6 %copy-start.2 = (f32[16,128]{1,0:T(8,128)}, f32[16,128]{1,0:T(8,128)S(1)}, u32[]{:S(2)}) copy-start(f32[16,128]{1,0:T(8,128)S(1)} %get-tuple-element.9) | copy-start | bytes 24580
Sparse Core Ops, SparseCore 0:
  12.4 737.9 reduce-scatter.1
  1105.5 285.0 all-gather.1
where the time goes:
time: 1400 us
  waiting for transfers between devices  1020 us (73%)
  blocking collectives  353 us (25%)
  between operations  14.1 us (1%)
    reduce_scatter x1, waiting for transfers between devices, per_device(): lax.psum_scatter(decoded, 'replica', scatter_dimension=1, tiled=True)  738 us
    all_gather x1, blocking collectives, per_device(): full_base = lax.all_gather(new_base, 'replica', axis=1, tiled=True)  353 us
    all_gather x1, waiting for transfers between devices, per_device(): merged_fragment = lax.all_gather(blended, 'fsdp', axis=0, tiled=True)  285 us
  transfers between devices with their start and end apart: 2, of which 2 were waited for; matrix products, arithmetic and copies ran while one was open for 0% of the time, Pallas kernels for 0%

commit v1 on v0

v1 whole, which is shorter than its diff:
```python
import jax
import jax.numpy as jnp
from jax import lax
from jax.experimental import pallas as pl
from jax.experimental.pallas import tpu as pltpu
from jax.sharding import PartitionSpec as P

MESH = pl.DeviceIdType.MESH
T = 128
BLOCK = 32


def kernel(
    local, base, mom, out, new_base, new_mom,
    dec, rx, p1, rb, p2, ra, nbh, nbbuf, zbuf,
    bulk_s, bulk_r, red_s, red_r, gat_s, gat_r, y_s, y_r, sib_s, sib_r,
):
    rep, fs = lax.axis_index("replica"), lax.axis_index("fsdp")
    x, zl = rep // 16, rep % 16
    a, b = zl // 4, zl % 4
    y, zh, core = fs // 4, (fs // 2) % 2, fs % 2

    def at_x(d):
        return (((x + d) % 4) * 16 + zl, fs)

    def at_a(d):
        return (x * 16 + ((a + d) % 4) * 4 + b, fs)

    def at_b(d):
        return (x * 16 + a * 4 + (b + d) % 4, fs)

    def at_y(d):
        return (rep, ((y + d) % 4) * 4 + zh * 2 + core)

    half = (rep, y * 4 + (1 - zh) * 2 + core)
    sibling = (rep, y * 4 + zh * 2 + (1 - core))

    barrier = pltpu.get_barrier_semaphore()
    peers = [f(d) for f in (at_x, at_a, at_b, at_y) for d in (1, 2, 3)]
    for peer in peers + [half, sibling]:
        pl.semaphore_signal(barrier, inc=1, device_id=peer, device_id_type=MESH)

    lane = lax.broadcasted_iota(jnp.int32, (16, T), 1)
    upper = [(lane // s) % 2 == 1 for s in (1, 2, 4, 8, 16)]

    def encode(q, carry):
        for i in range(4):
            for j in range(4):
                cols = pl.ds(pl.multiple_of(q * 2048 + (i * 4 + j) * T, T), T)
                delta = base[:, cols] - local[:, cols].astype(jnp.float32)
                most = jnp.abs(delta)
                for k, s in enumerate((1, 2, 4, 8, 16)):
                    other = jnp.where(
                        upper[k], pltpu.roll(most, s, 1), pltpu.roll(most, T - s, 1)
                    )
                    most = jnp.maximum(most, other)
                scale = (jnp.maximum(most, 1.0) / 6.0).astype(jnp.bfloat16)
                bound = 4.0 * scale.astype(jnp.float32)
                dec[q, j, i] = jnp.clip(delta, -bound, bound).astype(jnp.bfloat16)
        return carry

    lax.fori_loop(0, 4, encode, 0)
    pl.semaphore_wait(barrier, 14)

    def remote(src, dst, s, r, to):
        copy = pltpu.make_async_remote_copy(
            src_ref=src, dst_ref=dst, send_sem=s, recv_sem=r,
            device_id=to, device_id_type=MESH,
        )
        copy.start()
        return copy

    sent = []

    def exchange(copies):
        for copy in copies:
            copy.wait_recv()
        sent.extend(copies)

    x_copies = [
        remote(dec.at[(x + d) % 4], rx.at[d - 1], red_s.at[d - 1], red_r.at[d - 1], at_x(d))
        for d in (1, 2, 3)
    ]
    bulk = []
    for q in range(4):
        cols = pl.ds(pl.multiple_of(((x + q) % 4) * 2048, 2048), 2048)
        bulk.append(remote(local.at[:, cols], zbuf.at[:, cols], bulk_s.at[q], bulk_r.at[q], half))
    exchange(x_copies)

    def sum_x(j, carry):
        for i in range(4):
            total = dec[x, j, i].astype(jnp.float32)
            for d in range(3):
                total = total + rx[d, j, i].astype(jnp.float32)
            p1[j, i] = total.astype(jnp.bfloat16)
        return carry

    lax.fori_loop(0, 4, sum_x, 0)
    exchange([
        remote(p1.at[(b + d) % 4], rb.at[d - 1], red_s.at[2 + d], red_r.at[2 + d], at_b(d))
        for d in (1, 2, 3)
    ])
    for i in range(4):
        total = p1[b, i].astype(jnp.float32)
        for d in range(3):
            total = total + rb[d, i].astype(jnp.float32)
        p2[i] = total.astype(jnp.bfloat16)
    exchange([
        remote(p2.at[(a + d) % 4], ra.at[d - 1], red_s.at[5 + d], red_r.at[5 + d], at_a(d))
        for d in (1, 2, 3)
    ])
    total = p2[a].astype(jnp.float32)
    for d in range(3):
        total = total + ra[d].astype(jnp.float32)
    grad = total / 64.0
    momentum = 0.9 * mom[...] + grad
    own = base[:, pl.ds(pl.multiple_of(rep * T, T), T)]
    updated = own - 0.7 * (grad + 0.9 * momentum)
    new_mom[...] = momentum
    new_base[...] = updated
    nbh[...] = updated.astype(jnp.bfloat16)
    nbbuf[x, b, a, zh] = updated.astype(jnp.bfloat16)

    exchange([remote(nbh, nbbuf.at[x, b, a, zh], gat_s.at[0], gat_r.at[0], half)])
    exchange([
        remote(nbbuf.at[x, b, a], nbbuf.at[x, b, a], gat_s.at[d], gat_r.at[d], at_a(d))
        for d in (1, 2, 3)
    ])
    exchange([
        remote(nbbuf.at[x, b], nbbuf.at[x, b], gat_s.at[3 + d], gat_r.at[3 + d], at_b(d))
        for d in (1, 2, 3)
    ])
    x_gather = [
        remote(nbbuf.at[x], nbbuf.at[x], gat_s.at[6 + d], gat_r.at[6 + d], at_x(d))
        for d in (1, 2, 3)
    ]

    def blend(q, rows, which):
        place = y * 4 + which * 2 + core
        for i in range(4):
            for j in range(4):
                cols = pl.ds(pl.multiple_of(q * 2048 + (i * 4 + j) * T, T), T)
                value = 0.5 * nbbuf[q, j, i, which].astype(jnp.float32)
                value = value + 0.5 * rows[:, cols].astype(jnp.float32)
                out[place, :, cols] = value.astype(jnp.bfloat16)

    def block(place, q):
        return out.at[place, :, pl.ds(pl.multiple_of(q * 2048, 2048), 2048)]

    y_copies, sib_copies = {}, {}

    def spread(k, q, n):
        which = zh if k == 0 else 1 - zh
        here = block(y * 4 + which * 2 + core, q)
        for d in (1, 2, 3):
            y_copies[k, n, d] = remote(here, here, y_s.at[k, n, d - 1], y_r.at[k, n, d - 1], at_y(d))
        sib_copies[k, n, 0] = remote(here, here, sib_s.at[k, n, 0], sib_r.at[k, n, 0], sibling)

    def relay(k, q, n):
        which = zh if k == 0 else 1 - zh
        for d in (1, 2, 3):
            y_copies[k, n, d].wait_recv()
            here = block(((y + 4 - d) % 4) * 4 + which * 2 + core, q)
            sib_copies[k, n, d] = remote(here, here, sib_s.at[k, n, d], sib_r.at[k, n, d], sibling)

    order = [(x + 4 - d) % 4 for d in range(4)]
    for n in range(4):
        if n > 0:
            x_gather[n - 1].wait_recv()
        blend(order[n], local, zh)
        spread(0, order[n], n)
    landing = [0, 3, 2, 1]
    for n in range(4):
        bulk[landing[n]].wait_recv()
        blend(order[n], zbuf, 1 - zh)
        spread(1, order[n], n)
        relay(0, order[n], n)
    for n in range(4):
        relay(1, order[n], n)
    for k in range(2):
        for n in range(4):
            for d in range(4):
                sib_copies[k, n, d].wait()
            for d in (1, 2, 3):
                y_copies[k, n, d].wait_send()
    for copy in sent + bulk + x_gather:
        copy.wait_send()


def per_device(local_weights, base_weights, momentum):
    bf16, dma = jnp.bfloat16, pltpu.SemaphoreType.DMA
    vmem = pl.BlockSpec(memory_space=pltpu.VMEM)
    merged, new_base, new_momentum = pl.pallas_call(
        kernel,
        out_shape=(
            jax.ShapeDtypeStruct((16, 16, 8192), bf16),
            jax.ShapeDtypeStruct((16, T), jnp.float32),
            jax.ShapeDtypeStruct((16, T), jnp.float32),
        ),
        in_specs=[vmem] * 3,
        out_specs=(vmem,) * 3,
        scratch_shapes=[
            pltpu.VMEM((4, 4, 4, 16, T), bf16),
            pltpu.VMEM((3, 4, 4, 16, T), bf16),
            pltpu.VMEM((4, 4, 16, T), bf16),
            pltpu.VMEM((3, 4, 16, T), bf16),
            pltpu.VMEM((4, 16, T), bf16),
            pltpu.VMEM((3, 16, T), bf16),
            pltpu.VMEM((16, T), bf16),
            pltpu.VMEM((4, 4, 4, 2, 16, T), bf16),
            pltpu.VMEM((16, 8192), bf16),
            dma((4,)), dma((4,)), dma((9,)), dma((9,)), dma((10,)), dma((10,)),
            dma((2, 4, 3)), dma((2, 4, 3)), dma((2, 4, 4)), dma((2, 4, 4)),
        ],
        compiler_params=pltpu.CompilerParams(
            collective_id=0, has_side_effects=True, vmem_limit_bytes=24 * 2**20
        ),
    )(local_weights[0], base_weights, momentum)
    return merged.reshape(1, 256, 8192), new_base, new_momentum


def solution(mesh):
    in_specs = (P("replica", "fsdp", None), P("fsdp", None), P("fsdp", "replica"))
    out_specs = (P("replica", None, None), P("fsdp", "replica"), P("fsdp", "replica"))
    return jax.shard_map(
        per_device, mesh=mesh, in_specs=in_specs, out_specs=out_specs, check_vma=False
    )
```

time: 1400 us -> 145 us (0.10)
  waiting for transfers between devices: 1020 us -> 0 us
  blocking collectives: 353 us -> 0 us
  Pallas kernels: 0 us -> 138 us
    reduce_scatter x1 -> x0, waiting for transfers between devices: 738 us -> none  [per_device(): lax.psum_scatter(decoded, 'replica', scatter_dimension=1, tiled=True)]
    all_gather x1 -> x0, blocking collectives: 353 us -> none  [per_device(): full_base = lax.all_gather(new_base, 'replica', axis=1, tiled=True)]
    all_gather x1 -> x0, waiting for transfers between devices: 285 us -> none  [per_device(): merged_fragment = lax.all_gather(blended, 'fsdp', axis=0, tiled=True)]
    pallas_call x0 -> x1, Pallas kernels: none -> 138 us  [per_device(): pl.pallas_call(kernel, out_shape=(jax.ShapeDtypeStruct((16, 16, 8192), bf...]
  transfers between devices with their start and end apart: 2 -> 0, of which waited for: 2 -> 0; matrix products, arithmetic and copies ran while one was open for 0% -> 0% of each run, Pallas kernels for 0% -> 0%
where the time goes in v1:
time: 145 us
  Pallas kernels  138 us (95%)
  local copies, waits for them, and re-layouts  5.89 us (4%)
    pallas_call x1, Pallas kernels, per_device(): pl.pallas_call(kernel, out_shape=(jax.ShapeDtypeStruct((16, 16, 8192), bf...  138 us
    unnamed x9, local copies, waits for them, and re-layouts  5.89 us

profile of v1, /device:TPU:1, one launch (start us, length us, event | category | flops | bytes accessed | tf_op | source)
XLA Modules:
  0.0 145.0 jit_solution(9085254856696489773)
XLA Ops:
  0.6 0.0 copy-start
  0.6 1.0 copy-done
  1.7 0.0 copy-start.1
  1.7 0.9 copy-done.1
  2.6 0.0 copy-start.2
  2.6 0.7 copy-done.2
  3.3 138.5 %shard_map.58 = (bf16[16,16,8192]{2,1,0:T(8,128)(2,1)S(1)}, f32[16,128]{1,0:T(8,128)S(1)}, f32[16,128]{1,0:T(8,128)S(1)}) custom-call(bf16[16,8192]{1,0:T(8,128)(2,1)S(1)} %bitcast.3, f32[16,8192]{1,0:T(8,128)S(1)} %copy-done, f32[16,128]{1,0:T(8,128)S(1)} %copy-done.2), custom_call_target="tpu_custom_call" | custom-call | tf_op jit(solution)/shard_map/pallas_call | solution.py:193
  141.8 2.0 %copy.9 = bf16[1,256,8192]{2,1,0:T(8,128)(2,1)} copy(bf16[1,256,8192]{2,1,0:T(8,128)(2,1)S(1)} %bitcast.2) | data formatting | bytes 8388608
  143.8 0.6 copy.10
  144.4 0.6 copy.11
Async XLA Ops:
  0.6 1.0 copy-start
  1.7 0.9 copy-start.1
  2.6 0.7 copy-start.2

commit v2 on v1

v2 whole, which is shorter than its diff:
```python
import jax
import jax.numpy as jnp
from jax import lax
from jax.experimental import pallas as pl
from jax.experimental.pallas import tpu as pltpu
from jax.sharding import PartitionSpec as P

MESH = pl.DeviceIdType.MESH
T = 128
LEG = 4
CUT = ((0, 1), (2, 3), (0, 1), (2, 3))


def kernel(
    local, base, mom, out, new_base, new_mom,
    dec, rx, p1, rb, p2, ra, nbh, mine, theirs, ring,
    ring_s, ring_r, red_s, red_r, gat_s, gat_r, far_s, far_r, y_s, y_r, sib_s, sib_r, known,
):
    rep, fs = lax.axis_index("replica"), lax.axis_index("fsdp")
    x, zl = rep // 16, rep % 16
    a, b = zl // 4, zl % 4
    y, zh, core = fs // 4, (fs // 2) % 2, fs % 2

    def at_x(d):
        return (((x + d) % 4) * 16 + zl, fs)

    def at_a(d):
        return (x * 16 + ((a + d) % 4) * 4 + b, fs)

    def at_b(d):
        return (x * 16 + a * 4 + (b + d) % 4, fs)

    def at_y(d):
        return (rep, ((y + d) % 4) * 4 + zh * 2 + core)

    def far(d):
        return (x * 16 + ((a + d) % 4) * 4 + b, y * 4 + (1 - zh) * 2 + core)

    def along(d):
        z = (zh * 16 + zl + 32 + (LEG if d == 0 else -LEG)) % 32
        return (x * 16 + z % 16, y * 4 + (z // 16) * 2 + core)

    sibling = (rep, y * 4 + zh * 2 + (1 - core))

    barrier = pltpu.get_barrier_semaphore()
    peers = [f(d) for f in (at_x, at_b, at_y) for d in (1, 2, 3)] + [along(0), along(1), sibling]
    for peer in peers:
        pl.semaphore_signal(barrier, inc=1, device_id=peer, device_id_type=MESH)

    lane = lax.broadcasted_iota(jnp.int32, (16, T), 1)
    upper = [(lane // s) % 2 == 1 for s in (1, 2, 4, 8, 16)]

    def encode(q, carry):
        for i in range(4):
            for j in range(4):
                cols = pl.ds(pl.multiple_of(q * 2048 + (i * 4 + j) * T, T), T)
                delta = base[:, cols] - local[:, cols].astype(jnp.float32)
                most = jnp.abs(delta)
                for k, s in enumerate((1, 2, 4, 8, 16)):
                    other = jnp.where(
                        upper[k], pltpu.roll(most, s, 1), pltpu.roll(most, T - s, 1)
                    )
                    most = jnp.maximum(most, other)
                scale = (jnp.maximum(most, 1.0) / 6.0).astype(jnp.bfloat16)
                bound = 4.0 * scale.astype(jnp.float32)
                dec[q, j, i] = jnp.clip(delta, -bound, bound).astype(jnp.bfloat16)
        return carry

    lax.fori_loop(0, 4, encode, 0)
    pl.semaphore_wait(barrier, 12)

    def remote(src, dst, s, r, to):
        copy = pltpu.make_async_remote_copy(
            src_ref=src, dst_ref=dst, send_sem=s, recv_sem=r,
            device_id=to, device_id_type=MESH,
        )
        copy.start()
        return copy

    sent = []

    def arrived(copies):
        for copy in copies:
            copy.wait_recv()
        sent.extend(copies)

    def tell(n):
        for d in (0, 1):
            pl.semaphore_signal(known.at[n], inc=1, device_id=along(d), device_id_type=MESH)

    order = [(x + 4 - d) % 4 for d in range(4)]
    legs = {}

    def forward(k, c):
        for d in (0, 1):
            if k == 0:
                source = local.at[:, pl.ds(pl.multiple_of(order[c] * 2048 + d * 1024, 1024), 1024)]
            else:
                legs[k - 1, d, c].wait_recv()
                source = ring.at[k - 1, d, c]
            legs[k, d, c] = remote(source, ring.at[k, d, c], ring_s.at[k, d, c], ring_r.at[k, d, c], along(d))

    copies = [
        remote(dec.at[(x + d) % 4], rx.at[d - 1], red_s.at[d - 1], red_r.at[d - 1], at_x(d))
        for d in (1, 2, 3)
    ]
    for c in range(4):
        forward(0, c)
    tell(0)
    arrived(copies)

    def sum_x(j, carry):
        for i in range(4):
            total = dec[x, j, i].astype(jnp.float32)
            for d in range(3):
                total = total + rx[d, j, i].astype(jnp.float32)
            p1[j, i] = total.astype(jnp.bfloat16)
        return carry

    lax.fori_loop(0, 4, sum_x, 0)
    copies = [
        remote(p1.at[(b + d) % 4], rb.at[d - 1], red_s.at[2 + d], red_r.at[2 + d], at_b(d))
        for d in (1, 2, 3)
    ]
    pl.semaphore_wait(known.at[0], 2)
    tell(1)
    arrived(copies)
    for i in range(4):
        total = p1[b, i].astype(jnp.float32)
        for d in range(3):
            total = total + rb[d, i].astype(jnp.float32)
        p2[i] = total.astype(jnp.bfloat16)
    pl.semaphore_wait(known.at[1], 2)
    tell(2)
    copies = [
        remote(p2.at[(a + d) % 4], ra.at[d - 1], red_s.at[5 + d], red_r.at[5 + d], at_a(d))
        for d in (1, 2, 3)
    ]
    for c in CUT[0]:
        forward(1, c)
    pl.semaphore_wait(known.at[2], 2)
    arrived(copies)
    total = p2[a].astype(jnp.float32)
    for d in range(3):
        total = total + ra[d].astype(jnp.float32)
    grad = total / 64.0
    momentum = 0.9 * mom[...] + grad
    own = base[:, pl.ds(pl.multiple_of(rep * T, T), T)]
    updated = own - 0.7 * (grad + 0.9 * momentum)
    new_mom[...] = momentum
    new_base[...] = updated
    nbh[...] = updated.astype(jnp.bfloat16)

    near_a = [remote(nbh, mine.at[x, b, a], gat_s.at[d - 1], gat_r.at[d - 1], at_a(d)) for d in (1, 2, 3)]
    far_a = [remote(nbh, theirs.at[x, b, a], far_s.at[6 + d], far_r.at[6 + d], far(d)) for d in range(4)]
    mine[x, b, a] = updated.astype(jnp.bfloat16)
    for c in CUT[1]:
        forward(1, c)
    arrived(near_a)

    def to_b(which, s, r):
        return [remote(which.at[x, b], which.at[x, b], s.at[d - 1], r.at[d - 1], at_b(d)) for d in (1, 2, 3)]

    def to_x(which, s, r):
        return [remote(which.at[x], which.at[x], s.at[2 + d], r.at[2 + d], at_x(d)) for d in (1, 2, 3)]

    near_b = to_b(mine, gat_s.at[pl.ds(3, 6)], gat_r.at[pl.ds(3, 6)])
    for c in CUT[2]:
        forward(2, c)
    arrived(far_a)
    far_b = to_b(theirs, far_s, far_r)
    arrived(near_b)
    near_x = to_x(mine, gat_s.at[pl.ds(3, 6)], gat_r.at[pl.ds(3, 6)])
    for c in CUT[3]:
        forward(2, c)
    arrived(far_b)
    far_x = to_x(theirs, far_s, far_r)

    def blend(which, q, i, rows, cols, place, at):
        for j in range(4):
            value = 0.5 * which[q, j, i].astype(jnp.float32)
            value = value + 0.5 * rows[:, cols(j)].astype(jnp.float32)
            out[place, :, pl.ds(pl.multiple_of(at + j * T, T), T)] = value.astype(jnp.bfloat16)

    y_copies, sib_copies = {}, {}

    def spread(m, which, at, wide):
        here = out.at[y * 4 + which * 2 + core, :, pl.ds(pl.multiple_of(at, 1024), wide)]
        for d in (1, 2, 3):
            y_copies[m, d] = remote(here, here, y_s.at[m, d - 1], y_r.at[m, d - 1], at_y(d))
        sib_copies[m, 0] = remote(here, here, sib_s.at[m, 0], sib_r.at[m, 0], sibling)

    def relay(m, which, at, wide):
        for d in (1, 2, 3):
            y_copies[m, d].wait_recv()
            place = ((y + 4 - d) % 4) * 4 + which * 2 + core
            here = out.at[place, :, pl.ds(pl.multiple_of(at, 1024), wide)]
            sib_copies[m, d] = remote(here, here, sib_s.at[m, d], sib_r.at[m, d], sibling)

    for n in range(4):
        if n > 0:
            near_x[n - 1].wait_recv()
        at = order[n] * 2048
        for i in range(4):
            blend(
                mine, order[n], i, local,
                lambda j: pl.ds(pl.multiple_of(at + (i * 4 + j) * T, T), T),
                y * 4 + zh * 2 + core, at + i * 512,
            )
        spread(n, zh, at, 2048)
        forward(3, n)
    for n in range(4):
        if n > 0:
            far_x[n - 1].wait_recv()
        for d in (0, 1):
            legs[3, d, n].wait_recv()
            at = order[n] * 2048 + d * 1024
            for i in (0, 1):
                blend(
                    theirs, order[n], d * 2 + i, ring.at[3, d, n],
                    lambda j: pl.ds((i * 4 + j) * T, T),
                    y * 4 + (1 - zh) * 2 + core, at + i * 512,
                )
            spread(4 + n * 2 + d, 1 - zh, at, 1024)
        relay(n, zh, order[n] * 2048, 2048)
    for n in range(4):
        for d in (0, 1):
            relay(4 + n * 2 + d, 1 - zh, order[n] * 2048 + d * 1024, 1024)
    for copy in sib_copies.values():
        copy.wait()
    for copy in [*y_copies.values(), *legs.values(), *sent, *near_x, *far_x]:
        copy.wait_send()


def per_device(local_weights, base_weights, momentum):
    bf16, dma = jnp.bfloat16, pltpu.SemaphoreType.DMA
    vmem = pl.BlockSpec(memory_space=pltpu.VMEM)
    merged, new_base, new_momentum = pl.pallas_call(
        kernel,
        out_shape=(
            jax.ShapeDtypeStruct((16, 16, 8192), bf16),
            jax.ShapeDtypeStruct((16, T), jnp.float32),
            jax.ShapeDtypeStruct((16, T), jnp.float32),
        ),
        in_specs=[vmem] * 3,
        out_specs=(vmem,) * 3,
        scratch_shapes=[
            pltpu.VMEM((4, 4, 4, 16, T), bf16),
            pltpu.VMEM((3, 4, 4, 16, T), bf16),
            pltpu.VMEM((4, 4, 16, T), bf16),
            pltpu.VMEM((3, 4, 16, T), bf16),
            pltpu.VMEM((4, 16, T), bf16),
            pltpu.VMEM((3, 16, T), bf16),
            pltpu.VMEM((16, T), bf16),
            pltpu.VMEM((4, 4, 4, 16, T), bf16),
            pltpu.VMEM((4, 4, 4, 16, T), bf16),
            pltpu.VMEM((4, 2, 4, 16, 1024), bf16),
            dma((4, 2, 4)), dma((4, 2, 4)), dma((9,)), dma((9,)), dma((9,)), dma((9,)), dma((10,)), dma((10,)),
            dma((12, 3)), dma((12, 3)), dma((12, 4)), dma((12, 4)), pltpu.SemaphoreType.REGULAR((3,)),
        ],
        compiler_params=pltpu.CompilerParams(
            collective_id=0, has_side_effects=True, vmem_limit_bytes=24 * 2**20
        ),
    )(local_weights[0], base_weights, momentum)
    return merged.reshape(1, 256, 8192), new_base, new_momentum


def solution(mesh):
    in_specs = (P("replica", "fsdp", None), P("fsdp", None), P("fsdp", "replica"))
    out_specs = (P("replica", None, None), P("fsdp", "replica"), P("fsdp", "replica"))
    return jax.shard_map(
        per_device, mesh=mesh, in_specs=in_specs, out_specs=out_specs, check_vma=False
    )
```

time: 145 us -> 104 us (0.72)
  the two profiles are of different devices: /device:TPU:1 before, /device:TPU:103 now
where the time goes in v2:
time: 104 us
  Pallas kernels  97.3 us (94%)
  local copies, waits for them, and re-layouts  5.89 us (6%)
    pallas_call x1, Pallas kernels, per_device(): pl.pallas_call(kernel, out_shape=(jax.ShapeDtypeStruct((16, 16, 8192), bf...  97.3 us
    unnamed x9, local copies, waits for them, and re-layouts  5.89 us

profile of v2, /device:TPU:103, one launch (start us, length us, event | category | flops | bytes accessed | tf_op | source)
XLA Modules:
  0.0 103.8 jit_solution(15137358671252270478)
XLA Ops:
  0.6 0.0 copy-start
  0.6 1.0 copy-done
  1.7 0.0 copy-start.1
  1.7 0.9 copy-done.1
  2.6 0.0 copy-start.2
  2.6 0.7 copy-done.2
  3.3 97.3 %shard_map.58 = (bf16[16,16,8192]{2,1,0:T(8,128)(2,1)S(1)}, f32[16,128]{1,0:T(8,128)S(1)}, f32[16,128]{1,0:T(8,128)S(1)}) custom-call(bf16[16,8192]{1,0:T(8,128)(2,1)S(1)} %bitcast.3, f32[16,8192]{1,0:T(8,128)S(1)} %copy-done, f32[16,128]{1,0:T(8,128)S(1)} %copy-done.2), custom_call_target="tpu_custom_call" | custom-call | tf_op jit(solution)/shard_map/pallas_call | solution.py:238
  100.6 2.0 %copy.9 = bf16[1,256,8192]{2,1,0:T(8,128)(2,1)} copy(bf16[1,256,8192]{2,1,0:T(8,128)(2,1)S(1)} %bitcast.2) | data formatting | bytes 8388608
  102.6 0.6 copy.10
  103.2 0.6 copy.11
Async XLA Ops:
  0.6 1.0 %copy-start = (f32[16,8192]{1,0:T(8,128)S(1)}, f32[16,8192]{1,0:T(8,128)}, u32[]{:S(2)}) copy-start(f32[16,8192]{1,0:T(8,128)} %base.1) | copy-start | bytes 1572868
  1.7 0.9 copy-start.1
  2.6 0.7 copy-start.2

commit v3 on v2

--- a/solution.py
+++ b/solution.py
@@ -7,12 +7,19 @@
 
 MESH = pl.DeviceIdType.MESH
 T = 128
-LEG = 4
-CUT = ((0, 1), (2, 3), (0, 1), (2, 3))
+LEG = 2
+LEGS = 16 // LEG
+PLAN = (
+    "1.0", "1.1", "x", "1.2", "1.3", "b", "2.0", "2.1", "2.2", "2.3", "3.0", "3.1", "a", "3.2", "3.3", "4.0",
+    "4.1", "na", "4.2", "4.3", "5.0", "fa", "5.1", "nb", "5.2", "5.3", "fb", "6.0", "m0", "6.1", "m1", "6.2",
+    "6.3", "m2", "7.0", "m3", "7.1", "7.2", "7.3",
+)
+STRAIGHT = 12
 
 
 def kernel(
-    local, base, mom, out, new_base, new_mom,
+    local_h, base_h, mom_h, out, new_base, new_mom,
+    local, base, mom, in_sem,
     dec, rx, p1, rb, p2, ra, nbh, mine, theirs, ring,
     ring_s, ring_r, red_s, red_r, gat_s, gat_r, far_s, far_r, y_s, y_r, sib_s, sib_r, known,
 ):
@@ -30,22 +37,32 @@
     def at_b(d):
         return (x * 16 + a * 4 + (b + d) % 4, fs)
 
-    def at_y(d):
-        return (rep, ((y + d) % 4) * 4 + zh * 2 + core)
+    def at_y(d, which=core):
+        return (rep, ((y + d) % 4) * 4 + zh * 2 + which)
 
     def far(d):
         return (x * 16 + ((a + d) % 4) * 4 + b, y * 4 + (1 - zh) * 2 + core)
 
-    def along(d):
-        z = (zh * 16 + zl + 32 + (LEG if d == 0 else -LEG)) % 32
+    def along(d, n):
+        z = (zh * 16 + zl + 32 + (n if d == 0 else -n)) % 32
         return (x * 16 + z % 16, y * 4 + (z // 16) * 2 + core)
 
     sibling = (rep, y * 4 + zh * 2 + (1 - core))
 
     barrier = pltpu.get_barrier_semaphore()
-    peers = [f(d) for f in (at_x, at_b, at_y) for d in (1, 2, 3)] + [along(0), along(1), sibling]
+    peers = [f(d) for f in (at_x, at_b, at_y) for d in (1, 2, 3)] + [along(d, n) for d in (0, 1) for n in {LEG, 4}] + [sibling]
+    peers = peers + [at_y(d, 1 - core) for d in (1, 2, 3)]
     for peer in peers:
         pl.semaphore_signal(barrier, inc=1, device_id=peer, device_id_type=MESH)
+
+    loads = [
+        pltpu.make_async_copy(source, target, in_sem.at[n])
+        for n, (source, target) in enumerate(((base_h, base), (local_h, local), (mom_h, mom)))
+    ]
+    for load in loads:
+        load.start()
+    for load in loads:
+        load.wait()
 
     lane = lax.broadcasted_iota(jnp.int32, (16, T), 1)
     upper = [(lane // s) % 2 == 1 for s in (1, 2, 4, 8, 16)]
@@ -67,7 +84,7 @@
         return carry
 
     lax.fori_loop(0, 4, encode, 0)
-    pl.semaphore_wait(barrier, 12)
+    pl.semaphore_wait(barrier, len(peers))
 
     def remote(src, dst, s, r, to):
         copy = pltpu.make_async_remote_copy(
@@ -86,7 +103,7 @@
 
     def tell(n):
         for d in (0, 1):
-            pl.semaphore_signal(known.at[n], inc=1, device_id=along(d), device_id_type=MESH)
+            pl.semaphore_signal(known.at[n], inc=1, device_id=along(d, 4), device_id_type=MESH)
 
     order = [(x + 4 - d) % 4 for d in range(4)]
     legs = {}
@@ -98,7 +115,7 @@
             else:
                 legs[k - 1, d, c].wait_recv()
                 source = ring.at[k - 1, d, c]
-            legs[k, d, c] = remote(source, ring.at[k, d, c], ring_s.at[k, d, c], ring_r.at[k, d, c], along(d))
+            legs[k, d, c] = remote(source, ring.at[k, d, c], ring_s.at[k, d, c], ring_r.at[k, d, c], along(d, LEG))
 
     copies = [
         remote(dec.at[(x + d) % 4], rx.at[d - 1], red_s.at[d - 1], red_r.at[d - 1], at_x(d))
@@ -107,7 +124,6 @@
     for c in range(4):
         forward(0, c)
     tell(0)
-    arrived(copies)
 
     def sum_x(j, carry):
         for i in range(4):
@@ -117,64 +133,11 @@
             p1[j, i] = total.astype(jnp.bfloat16)
         return carry
 
-    lax.fori_loop(0, 4, sum_x, 0)
-    copies = [
-        remote(p1.at[(b + d) % 4], rb.at[d - 1], red_s.at[2 + d], red_r.at[2 + d], at_b(d))
-        for d in (1, 2, 3)
-    ]
-    pl.semaphore_wait(known.at[0], 2)
-    tell(1)
-    arrived(copies)
-    for i in range(4):
-        total = p1[b, i].astype(jnp.float32)
-        for d in range(3):
-            total = total + rb[d, i].astype(jnp.float32)
-        p2[i] = total.astype(jnp.bfloat16)
-    pl.semaphore_wait(known.at[1], 2)
-    tell(2)
-    copies = [
-        remote(p2.at[(a + d) % 4], ra.at[d - 1], red_s.at[5 + d], red_r.at[5 + d], at_a(d))
-        for d in (1, 2, 3)
-    ]
-    for c in CUT[0]:
-        forward(1, c)
-    pl.semaphore_wait(known.at[2], 2)
-    arrived(copies)
-    total = p2[a].astype(jnp.float32)
-    for d in range(3):
-        total = total + ra[d].astype(jnp.float32)
-    grad = total / 64.0
-    momentum = 0.9 * mom[...] + grad
-    own = base[:, pl.ds(pl.multiple_of(rep * T, T), T)]
-    updated = own - 0.7 * (grad + 0.9 * momentum)
-    new_mom[...] = momentum
-    new_base[...] = updated
-    nbh[...] = updated.astype(jnp.bfloat16)
-
-    near_a = [remote(nbh, mine.at[x, b, a], gat_s.at[d - 1], gat_r.at[d - 1], at_a(d)) for d in (1, 2, 3)]
-    far_a = [remote(nbh, theirs.at[x, b, a], far_s.at[6 + d], far_r.at[6 + d], far(d)) for d in range(4)]
-    mine[x, b, a] = updated.astype(jnp.bfloat16)
-    for c in CUT[1]:
-        forward(1, c)
-    arrived(near_a)
-
     def to_b(which, s, r):
         return [remote(which.at[x, b], which.at[x, b], s.at[d - 1], r.at[d - 1], at_b(d)) for d in (1, 2, 3)]
 
     def to_x(which, s, r):
         return [remote(which.at[x], which.at[x], s.at[2 + d], r.at[2 + d], at_x(d)) for d in (1, 2, 3)]
-
-    near_b = to_b(mine, gat_s.at[pl.ds(3, 6)], gat_r.at[pl.ds(3, 6)])
-    for c in CUT[2]:
-        forward(2, c)
-    arrived(far_a)
-    far_b = to_b(theirs, far_s, far_r)
-    arrived(near_b)
-    near_x = to_x(mine, gat_s.at[pl.ds(3, 6)], gat_r.at[pl.ds(3, 6)])
-    for c in CUT[3]:
-        forward(2, c)
-    arrived(far_b)
-    far_x = to_x(theirs, far_s, far_r)
 
     def blend(which, q, i, rows, cols, place, at):
         for j in range(4):
@@ -184,20 +147,28 @@
 
     y_copies, sib_copies = {}, {}
 
+    def straight(m):
+        return m >= STRAIGHT
+
     def spread(m, which, at, wide):
         here = out.at[y * 4 + which * 2 + core, :, pl.ds(pl.multiple_of(at, 1024), wide)]
         for d in (1, 2, 3):
             y_copies[m, d] = remote(here, here, y_s.at[m, d - 1], y_r.at[m, d - 1], at_y(d))
+        if straight(m):
+            for d in (1, 2, 3):
+                sib_copies[m, d] = remote(here, here, sib_s.at[m, d], sib_r.at[m, d], at_y(d, 1 - core))
         sib_copies[m, 0] = remote(here, here, sib_s.at[m, 0], sib_r.at[m, 0], sibling)
 
     def relay(m, which, at, wide):
         for d in (1, 2, 3):
             y_copies[m, d].wait_recv()
+            if straight(m):
+                continue
             place = ((y + 4 - d) % 4) * 4 + which * 2 + core
             here = out.at[place, :, pl.ds(pl.multiple_of(at, 1024), wide)]
             sib_copies[m, d] = remote(here, here, sib_s.at[m, d], sib_r.at[m, d], sibling)
 
-    for n in range(4):
+    def blend_mine(n, near_x):
         if n > 0:
             near_x[n - 1].wait_recv()
         at = order[n] * 2048
@@ -208,16 +179,84 @@
                 y * 4 + zh * 2 + core, at + i * 512,
             )
         spread(n, zh, at, 2048)
-        forward(3, n)
+
+    def step_x(copies):
+        arrived(copies)
+        lax.fori_loop(0, 4, sum_x, 0)
+        copies = [
+            remote(p1.at[(b + d) % 4], rb.at[d - 1], red_s.at[2 + d], red_r.at[2 + d], at_b(d))
+            for d in (1, 2, 3)
+        ]
+        pl.semaphore_wait(known.at[0], 2)
+        tell(1)
+        return copies
+
+    def step_b(copies):
+        arrived(copies)
+        for i in range(4):
+            total = p1[b, i].astype(jnp.float32)
+            for d in range(3):
+                total = total + rb[d, i].astype(jnp.float32)
+            p2[i] = total.astype(jnp.bfloat16)
+        pl.semaphore_wait(known.at[1], 2)
+        tell(2)
+        return [
+            remote(p2.at[(a + d) % 4], ra.at[d - 1], red_s.at[5 + d], red_r.at[5 + d], at_a(d))
+            for d in (1, 2, 3)
+        ]
+
+    def step_a(copies):
+        pl.semaphore_wait(known.at[2], 2)
+        arrived(copies)
+        total = p2[a].astype(jnp.float32)
+        for d in range(3):
+            total = total + ra[d].astype(jnp.float32)
+        grad = total / 64.0
+        momentum = 0.9 * mom[...] + grad
+        own = base[:, pl.ds(pl.multiple_of(rep * T, T), T)]
+        updated = own - 0.7 * (grad + 0.9 * momentum)
+        nbh[...] = updated.astype(jnp.bfloat16)
+        near = [remote(nbh, mine.at[x, b, a], gat_s.at[d - 1], gat_r.at[d - 1], at_a(d)) for d in (1, 2, 3)]
+        other = [remote(nbh, theirs.at[x, b, a], far_s.at[6 + d], far_r.at[6 + d], far(d)) for d in range(4)]
+        mine[x, b, a] = updated.astype(jnp.bfloat16)
+        new_mom[...] = momentum
+        new_base[...] = updated
+        return near, other
+
+    at = {"x": copies}
+    for step in PLAN:
+        if step == "x":
+            at["b"] = step_x(at["x"])
+        elif step == "b":
+            at["a"] = step_b(at["b"])
+        elif step == "a":
+            at["na"], at["fa"] = step_a(at["a"])
+        elif step == "na":
+            arrived(at["na"])
+            at["nb"] = to_b(mine, gat_s.at[pl.ds(3, 6)], gat_r.at[pl.ds(3, 6)])
+        elif step == "fa":
+            arrived(at["fa"])
+            at["fb"] = to_b(theirs, far_s, far_r)
+        elif step == "nb":
+            arrived(at["nb"])
+            near_x = to_x(mine, gat_s.at[pl.ds(3, 6)], gat_r.at[pl.ds(3, 6)])
+        elif step == "fb":
+            arrived(at["fb"])
+            far_x = to_x(theirs, far_s, far_r)
+        elif step[0] == "m":
+            blend_mine(int(step[1]), near_x)
+        else:
+            k, c = step.split(".")
+            forward(int(k), int(c))
     for n in range(4):
         if n > 0:
             far_x[n - 1].wait_recv()
         for d in (0, 1):
-            legs[3, d, n].wait_recv()
+            legs[LEGS - 1, d, n].wait_recv()
             at = order[n] * 2048 + d * 1024
             for i in (0, 1):
                 blend(
-                    theirs, order[n], d * 2 + i, ring.at[3, d, n],
+                    theirs, order[n], d * 2 + i, ring.at[LEGS - 1, d, n],
                     lambda j: pl.ds((i * 4 + j) * T, T),
                     y * 4 + (1 - zh) * 2 + core, at + i * 512,
                 )
@@ -242,9 +281,10 @@
             jax.ShapeDtypeStruct((16, T), jnp.float32),
             jax.ShapeDtypeStruct((16, T), jnp.float32),
         ),
-        in_specs=[vmem] * 3,
+        in_specs=[pl.BlockSpec(memory_space=pltpu.HBM)] * 3,
         out_specs=(vmem,) * 3,
         scratch_shapes=[
+            pltpu.VMEM((16, 8192), bf16), pltpu.VMEM((16, 8192), jnp.float32), pltpu.VMEM((16, T), jnp.float32), dma((3,)),
             pltpu.VMEM((4, 4, 4, 16, T), bf16),
             pltpu.VMEM((3, 4, 4, 16, T), bf16),
             pltpu.VMEM((4, 4, 16, T), bf16),
@@ -254,14 +294,14 @@
             pltpu.VMEM((16, T), bf16),
             pltpu.VMEM((4, 4, 4, 16, T), bf16),
             pltpu.VMEM((4, 4, 4, 16, T), bf16),
-            pltpu.VMEM((4, 2, 4, 16, 1024), bf16),
-            dma((4, 2, 4)), dma((4, 2, 4)), dma((9,)), dma((9,)), dma((9,)), dma((9,)), dma((10,)), dma((10,)),
+            pltpu.VMEM((LEGS, 2, 4, 16, 1024), bf16),
+            dma((LEGS, 2, 4)), dma((LEGS, 2, 4)), dma((9,)), dma((9,)), dma((9,)), dma((9,)), dma((10,)), dma((10,)),
             dma((12, 3)), dma((12, 3)), dma((12, 4)), dma((12, 4)), pltpu.SemaphoreType.REGULAR((3,)),
         ],
         compiler_params=pltpu.CompilerParams(
             collective_id=0, has_side_effects=True, vmem_limit_bytes=24 * 2**20
         ),
-    )(local_weights[0], base_weights, momentum)
+    )(*(pltpu.with_memory_space_constraint(v, pltpu.HBM) for v in (local_weights[0], base_weights, momentum)))
     return merged.reshape(1, 256, 8192), new_base, new_momentum
 
 

time: 104 us -> 96.9 us (0.932)
  the two profiles are of different devices: /device:TPU:103 before, /device:TPU:1 now
where the time goes in v3:
time: 96.9 us; the launch traced here: 96.7 us
  Pallas kernels  92.9 us (96%)
  local copies, waits for them, and re-layouts  3.21 us (3%)
    pallas_call x1, Pallas kernels, per_device(): pl.pallas_call(kernel, out_shape=(jax.ShapeDtypeStruct((16, 16, 8192), bf...  92.9 us
    unnamed x3, local copies, waits for them, and re-layouts  3.21 us

profile of v3, /device:TPU:1, one launch (start us, length us, event | category | flops | bytes accessed | tf_op | source)
XLA Modules:
  0.0 96.7 jit_solution(3714910237865563146)
XLA Ops:
  0.6 92.9 %shard_map.58 = (bf16[16,16,8192]{2,1,0:T(8,128)(2,1)S(1)}, f32[16,128]{1,0:T(8,128)S(1)}, f32[16,128]{1,0:T(8,128)S(1)}) custom-call(bf16[16,8192]{1,0:T(8,128)(2,1)} %bitcast.3, f32[16,8192]{1,0:T(8,128)} %base_h.1, f32[16,128]{1,0:T(8,128)} %mom_h.1), custom_call_target="tpu_custom_call" | custom-call | tf_op jit(solution)/shard_map/pallas_call | solution.py:277
  93.5 2.0 %copy.9 = bf16[1,256,8192]{2,1,0:T(8,128)(2,1)} copy(bf16[1,256,8192]{2,1,0:T(8,128)(2,1)S(1)} %bitcast.2) | data formatting | bytes 8388608
  95.5 0.6 copy.10
  96.1 0.6 copy.11

commit v4 on v3

--- a/solution.py
+++ b/solution.py
@@ -11,8 +11,8 @@
 LEGS = 16 // LEG
 PLAN = (
     "1.0", "1.1", "x", "1.2", "1.3", "b", "2.0", "2.1", "2.2", "2.3", "3.0", "3.1", "a", "3.2", "3.3", "4.0",
-    "4.1", "na", "4.2", "4.3", "5.0", "fa", "5.1", "nb", "5.2", "5.3", "fb", "6.0", "m0", "6.1", "m1", "6.2",
-    "6.3", "m2", "7.0", "m3", "7.1", "7.2", "7.3",
+    "4.1", "na", "4.2", "4.3", "5.0", "fa", "5.1", "nb", "5.2", "5.3", "fb", "6.0", "m0", "m1", "m2", "m3", "6.1",
+    "6.2", "6.3", "7.0", "7.1", "7.2", "7.3",
 )
 STRAIGHT = 12
 
@@ -261,7 +261,9 @@
                     y * 4 + (1 - zh) * 2 + core, at + i * 512,
                 )
             spread(4 + n * 2 + d, 1 - zh, at, 1024)
-        relay(n, zh, order[n] * 2048, 2048)
+        if n > 0:
+            relay(n - 1, zh, order[n - 1] * 2048, 2048)
+    relay(3, zh, order[3] * 2048, 2048)
     for n in range(4):
         for d in (0, 1):
             relay(4 + n * 2 + d, 1 - zh, order[n] * 2048 + d * 1024, 1024)

time: 96.9 us -> 96.5 us (level)
  no operation moved by 1% of the time
where the time goes in v4:
time: 96.5 us; the launch traced here: 96 us
  Pallas kernels  92.1 us (95%)
  local copies, waits for them, and re-layouts  3.21 us (3%)
    pallas_call x1, Pallas kernels, per_device(): pl.pallas_call(kernel, out_shape=(jax.ShapeDtypeStruct((16, 16, 8192), bf...  92.1 us
    unnamed x3, local copies, waits for them, and re-layouts  3.21 us

profile of v4, /device:TPU:1, one launch (start us, length us, event | category | flops | bytes accessed | tf_op | source)
XLA Modules:
  0.0 96.0 jit_solution(16825977984276480200)
XLA Ops:
  0.6 92.1 %shard_map.58 = (bf16[16,16,8192]{2,1,0:T(8,128)(2,1)S(1)}, f32[16,128]{1,0:T(8,128)S(1)}, f32[16,128]{1,0:T(8,128)S(1)}) custom-call(bf16[16,8192]{1,0:T(8,128)(2,1)} %bitcast.3, f32[16,8192]{1,0:T(8,128)} %base_h.1, f32[16,128]{1,0:T(8,128)} %mom_h.1), custom_call_target="tpu_custom_call" | custom-call | tf_op jit(solution)/shard_map/pallas_call | solution.py:279
  92.8 2.0 %copy.9 = bf16[1,256,8192]{2,1,0:T(8,128)(2,1)} copy(bf16[1,256,8192]{2,1,0:T(8,128)(2,1)S(1)} %bitcast.2) | data formatting | bytes 8388608
  94.8 0.6 copy.10
  95.4 0.6 copy.11

commit v5 on v4

--- a/solution.py
+++ b/solution.py
@@ -263,8 +263,11 @@
             spread(4 + n * 2 + d, 1 - zh, at, 1024)
         if n > 0:
             relay(n - 1, zh, order[n - 1] * 2048, 2048)
+        if n > 1:
+            for d in (0, 1):
+                relay(n * 2 + d, 1 - zh, order[n - 2] * 2048 + d * 1024, 1024)
     relay(3, zh, order[3] * 2048, 2048)
-    for n in range(4):
+    for n in (2, 3):
         for d in (0, 1):
             relay(4 + n * 2 + d, 1 - zh, order[n] * 2048 + d * 1024, 1024)
     for copy in sib_copies.values():

time: 96.5 us -> 96.5 us (level)
  no operation moved by 1% of the time
where the time goes in v5:
time: 96.5 us; the launch traced here: 96 us
  Pallas kernels  92.1 us (95%)
  local copies, waits for them, and re-layouts  3.21 us (3%)
    pallas_call x1, Pallas kernels, per_device(): pl.pallas_call(kernel, out_shape=(jax.ShapeDtypeStruct((16, 16, 8192), bf...  92.1 us
    unnamed x3, local copies, waits for them, and re-layouts  3.21 us

profile of v5, /device:TPU:1, one launch (start us, length us, event | category | flops | bytes accessed | tf_op | source)
XLA Modules:
  0.0 96.0 jit_solution(15651068784620542786)
XLA Ops:
  0.6 92.1 %shard_map.58 = (bf16[16,16,8192]{2,1,0:T(8,128)(2,1)S(1)}, f32[16,128]{1,0:T(8,128)S(1)}, f32[16,128]{1,0:T(8,128)S(1)}) custom-call(bf16[16,8192]{1,0:T(8,128)(2,1)} %bitcast.3, f32[16,8192]{1,0:T(8,128)} %base_h.1, f32[16,128]{1,0:T(8,128)} %mom_h.1), custom_call_target="tpu_custom_call" | custom-call | tf_op jit(solution)/shard_map/pallas_call | solution.py:282
  92.8 2.0 %copy.9 = bf16[1,256,8192]{2,1,0:T(8,128)(2,1)} copy(bf16[1,256,8192]{2,1,0:T(8,128)(2,1)S(1)} %bitcast.2) | data formatting | bytes 8388608
  94.8 0.6 copy.10
  95.4 0.6 copy.11
